TPU v7x, 128 devices: a whole 4x4x4 slice. The times are simulated.
128 devices in a mesh: lag: 4 (over y_hi, core), row: 32 (over y_lo, z, x).
Axes of the slice: x: 4, y: 4 (y_hi: 2, y_lo: 2; y = y_hi * 2 + y_lo), z: 4, core: 2. Of those that a mesh axis runs over, the one named last changes fastest.
Arguments:
- history: bfloat16 [64, 16, 16384], P('lag'), may hold values from -6 to 6
- tiles: bfloat16 [64, 128, 8, 128, 128], P('lag', 'row'), may hold values from -0.015625 to 0.015625
- columns: int32 [64, 128, 8], P('lag', 'row'), may hold values from 0 to 127
- counts: int32 [64, 128], P('lag', 'row'), may hold values from 1 to 8, as said below
- inverse: bfloat16 [128, 128, 128], P('row')
- excitation: float32 [16, 16, 16384], P(None, None, 'row'), may hold values from -6 to 6
Outputs:
- solutions: bfloat16 [16, 16, 16384], P(None, None, 'row')
Inputs may be any that keep to these rules, and one draw needn't show every extreme that they name: Slots 0 .. counts - 1 of a row block hold its tiles, the rest are padding; in every lag some row block fills all 8 slots.
All inputs are finite; a program needn't handle non-finite values.
Results may differ from a plain program's by a relative error of at most 0.0051.
Values may be sent and summed in bfloat16 or wider, within the bound.
A program may use at most 128 MiB of HBM per device.

v0:
```python
import jax
import jax.numpy as jnp
from jax import lax
from jax.sharding import PartitionSpec as P


def passed_along(block, axis, distance):
    devices = range(lax.axis_size(axis))
    route = [(i - distance, i) for i in devices if i - distance in devices]
    return lax.ppermute(block, axis, route)


def block_solve(field, blocks):
    pulses = field.shape[0]
    count = blocks.shape[0]
    tile = blocks.shape[1]
    rhs = field.astype(jnp.bfloat16).reshape(pulses, count, tile)
    solved = jnp.einsum("bij,pbj->pbi", blocks, rhs, preferred_element_type=jnp.float32)
    return solved.astype(jnp.bfloat16).reshape(pulses, count * tile)


def local(history, tiles, columns, counts, inverse, excitation):
    lag_dev, pulses, width = history.shape
    rb_dev = tiles.shape[1]
    kslots = tiles.shape[2]
    tile = tiles.shape[3]
    rows_dev = rb_dev * tile
    nblocks = width // tile
    steps = excitation.shape[0]
    lag_index = lax.axis_index("lag")
    keep = (jnp.arange(kslots)[None, None, :] < counts[:, :, None]).astype(jnp.bfloat16)
    slot_base = jnp.arange(lag_dev, dtype=jnp.int32)

    def advance(step, carry):
        buffer, solutions = carry
        slot_of = (slot_base - step) % lag_dev
        blocks = buffer.reshape(lag_dev, pulses, nblocks, tile)
        picked = blocks[slot_of[:, None, None], :, columns]
        picked = picked * keep[:, :, :, None, None]
        partial_value = jnp.einsum(
            "jbkic,jbkpc->pbi", tiles, picked, preferred_element_type=jnp.float32
        )
        partial_value = partial_value.reshape(pulses, rows_dev)
        own_field = lax.dynamic_index_in_dim(excitation, step, 0, keepdims=False)
        total = lax.psum(partial_value, "lag")
        solved = block_solve(own_field - total, inverse)
        solutions = lax.dynamic_update_index_in_dim(solutions, solved, step, 0)
        oldest = (lag_dev - 1 - step) % lag_dev
        last_entry = lax.dynamic_index_in_dim(buffer, oldest, 0, keepdims=False)
        newest_all = lax.all_gather(solved, "row", axis=1, tiled=True)
        arrived = passed_along(last_entry, "lag", 1)
        newest = jnp.where(lag_index == 0, newest_all, arrived)
        buffer = lax.dynamic_update_index_in_dim(buffer, newest, oldest, 0)
        return (buffer, solutions)

    empty = jnp.zeros((steps, pulses, rows_dev), jnp.bfloat16)
    final_buffer, solutions = lax.fori_loop(0, steps, advance, (history, empty))
    return solutions


def solution(mesh):
    return jax.shard_map(
        local,
        mesh=mesh,
        in_specs=(
            P("lag", None, None),
            P("lag", "row", None, None, None),
            P("lag", "row", None),
            P("lag", "row"),
            P("row", None, None),
            P(None, None, "row"),
        ),
        out_specs=P(None, None, "row"),
        check_vma=False,
    )
```

profile of v0, /device:TPU:25, one launch (start us, length us, event | category | flops | bytes accessed | tf_op | source)
XLA Modules:
  0.0 1973.7 jit_solution(7441602174500510733)
XLA Ops:
  7.7 1966.0 %while.18 = (s32[]{:T(128)}, bf16[16,16,16384]{2,1,0:T(8,128)(2,1)}, bf16[16,16,512]{2,1,0:T(8,128)(2,1)}, pred[]{:T(512)}, f32[16,16,512]{2,1,0:T(8,128)}, /*in...) while((s32[]{:T(128)}, ...), condition=%wide.region_2.3_spmd.clone, body=%wide.region_0.2_spmd.clone.sunk | while | flops 271880480 | bytes 45629644 | solution.py:57
  48.7 70.7 %all_gather.12 = bf16[16,16384]{1,0:T(8,128)(2,1)S(1)} all-gather(bf16[16,512]{1,0:T(8,128)(2,1)S(1)} %copy_bitcast_fusion.6), channel_id=1, replica_groups=mesh['lag'=4,'row'=32] {'row'}, dimensions={1}, use_global_device_ids=true | all-gather | bytes 540672 | tf_op jit(solution)/shard_map/while/body/eval_jaxpr/all_gather | solution.py:50
  177.7 64.4 %all_gather.12 = bf16[16,16384]{1,0:T(8,128)(2,1)S(1)} all-gather(bf16[16,512]{1,0:T(8,128)(2,1)S(1)} %copy_bitcast_fusion.6), channel_id=1, replica_groups=mesh['lag'=4,'row'=32] {'row'}, dimensions={1}, use_global_device_ids=true | all-gather | bytes 540672 | tf_op jit(solution)/shard_map/while/body/eval_jaxpr/all_gather | solution.py:50
  300.4 66.0 %all_gather.12 = bf16[16,16384]{1,0:T(8,128)(2,1)S(1)} all-gather(bf16[16,512]{1,0:T(8,128)(2,1)S(1)} %copy_bitcast_fusion.6), channel_id=1, replica_groups=mesh['lag'=4,'row'=32] {'row'}, dimensions={1}, use_global_device_ids=true | all-gather | bytes 540672 | tf_op jit(solution)/shard_map/while/body/eval_jaxpr/all_gather | solution.py:50
  392.3 30.9 %psum.16 = f32[16,512]{1,0:T(8,128)S(1)} all-reduce(f32[16,512]{1,0:T(8,128)S(1)} %bitcast.81), channel_id=1, replica_groups=mesh['lag'=4,'row'=32] {'lag'}, use_global_device_ids=true, to_apply=%region_1.1 | all-reduce | flops 8192 | bytes 65536 | tf_op jit(solution)/shard_map/while/body/eval_jaxpr/psum | solution.py:45
  424.8 64.5 %all_gather.12 = bf16[16,16384]{1,0:T(8,128)(2,1)S(1)} all-gather(bf16[16,512]{1,0:T(8,128)(2,1)S(1)} %copy_bitcast_fusion.6), channel_id=1, replica_groups=mesh['lag'=4,'row'=32] {'row'}, dimensions={1}, use_global_device_ids=true | all-gather | bytes 540672 | tf_op jit(solution)/shard_map/while/body/eval_jaxpr/all_gather | solution.py:50
  547.7 66.0 %all_gather.12 = bf16[16,16384]{1,0:T(8,128)(2,1)S(1)} all-gather(bf16[16,512]{1,0:T(8,128)(2,1)S(1)} %copy_bitcast_fusion.6), channel_id=1, replica_groups=mesh['lag'=4,'row'=32] {'row'}, dimensions={1}, use_global_device_ids=true | all-gather | bytes 540672 | tf_op jit(solution)/shard_map/while/body/eval_jaxpr/all_gather | solution.py:50
  639.5 30.9 %psum.16 = f32[16,512]{1,0:T(8,128)S(1)} all-reduce(f32[16,512]{1,0:T(8,128)S(1)} %bitcast.81), channel_id=1, replica_groups=mesh['lag'=4,'row'=32] {'lag'}, use_global_device_ids=true, to_apply=%region_1.1 | all-reduce | flops 8192 | bytes 65536 | tf_op jit(solution)/shard_map/while/body/eval_jaxpr/psum | solution.py:45
  672.0 64.5 %all_gather.12 = bf16[16,16384]{1,0:T(8,128)(2,1)S(1)} all-gather(bf16[16,512]{1,0:T(8,128)(2,1)S(1)} %copy_bitcast_fusion.6), channel_id=1, replica_groups=mesh['lag'=4,'row'=32] {'row'}, dimensions={1}, use_global_device_ids=true | all-gather | bytes 540672 | tf_op jit(solution)/shard_map/while/body/eval_jaxpr/all_gather | solution.py:50
  794.9 65.9 %all_gather.12 = bf16[16,16384]{1,0:T(8,128)(2,1)S(1)} all-gather(bf16[16,512]{1,0:T(8,128)(2,1)S(1)} %copy_bitcast_fusion.6), channel_id=1, replica_groups=mesh['lag'=4,'row'=32] {'row'}, dimensions={1}, use_global_device_ids=true | all-gather | bytes 540672 | tf_op jit(solution)/shard_map/while/body/eval_jaxpr/all_gather | solution.py:50
  886.7 31.0 %psum.16 = f32[16,512]{1,0:T(8,128)S(1)} all-reduce(f32[16,512]{1,0:T(8,128)S(1)} %bitcast.81), channel_id=1, replica_groups=mesh['lag'=4,'row'=32] {'lag'}, use_global_device_ids=true, to_apply=%region_1.1 | all-reduce | flops 8192 | bytes 65536 | tf_op jit(solution)/shard_map/while/body/eval_jaxpr/psum | solution.py:45
  919.3 64.5 %all_gather.12 = bf16[16,16384]{1,0:T(8,128)(2,1)S(1)} all-gather(bf16[16,512]{1,0:T(8,128)(2,1)S(1)} %copy_bitcast_fusion.6), channel_id=1, replica_groups=mesh['lag'=4,'row'=32] {'row'}, dimensions={1}, use_global_device_ids=true | all-gather | bytes 540672 | tf_op jit(solution)/shard_map/while/body/eval_jaxpr/all_gather | solution.py:50
  1042.2 65.9 %all_gather.12 = bf16[16,16384]{1,0:T(8,128)(2,1)S(1)} all-gather(bf16[16,512]{1,0:T(8,128)(2,1)S(1)} %copy_bitcast_fusion.6), channel_id=1, replica_groups=mesh['lag'=4,'row'=32] {'row'}, dimensions={1}, use_global_device_ids=true | all-gather | bytes 540672 | tf_op jit(solution)/shard_map/while/body/eval_jaxpr/all_gather | solution.py:50
  1133.9 31.0 %psum.16 = f32[16,512]{1,0:T(8,128)S(1)} all-reduce(f32[16,512]{1,0:T(8,128)S(1)} %bitcast.81), channel_id=1, replica_groups=mesh['lag'=4,'row'=32] {'lag'}, use_global_device_ids=true, to_apply=%region_1.1 | all-reduce | flops 8192 | bytes 65536 | tf_op jit(solution)/shard_map/while/body/eval_jaxpr/psum | solution.py:45
  1166.5 64.5 %all_gather.12 = bf16[16,16384]{1,0:T(8,128)(2,1)S(1)} all-gather(bf16[16,512]{1,0:T(8,128)(2,1)S(1)} %copy_bitcast_fusion.6), channel_id=1, replica_groups=mesh['lag'=4,'row'=32] {'row'}, dimensions={1}, use_global_device_ids=true | all-gather | bytes 540672 | tf_op jit(solution)/shard_map/while/body/eval_jaxpr/all_gather | solution.py:50
  1289.4 65.9 %all_gather.12 = bf16[16,16384]{1,0:T(8,128)(2,1)S(1)} all-gather(bf16[16,512]{1,0:T(8,128)(2,1)S(1)} %copy_bitcast_fusion.6), channel_id=1, replica_groups=mesh['lag'=4,'row'=32] {'row'}, dimensions={1}, use_global_device_ids=true | all-gather | bytes 540672 | tf_op jit(solution)/shard_map/while/body/eval_jaxpr/all_gather | solution.py:50
  1381.1 31.0 %psum.16 = f32[16,512]{1,0:T(8,128)S(1)} all-reduce(f32[16,512]{1,0:T(8,128)S(1)} %bitcast.81), channel_id=1, replica_groups=mesh['lag'=4,'row'=32] {'lag'}, use_global_device_ids=true, to_apply=%region_1.1 | all-reduce | flops 8192 | bytes 65536 | tf_op jit(solution)/shard_map/while/body/eval_jaxpr/psum | solution.py:45
  1413.7 64.5 %all_gather.12 = bf16[16,16384]{1,0:T(8,128)(2,1)S(1)} all-gather(bf16[16,512]{1,0:T(8,128)(2,1)S(1)} %copy_bitcast_fusion.6), channel_id=1, replica_groups=mesh['lag'=4,'row'=32] {'row'}, dimensions={1}, use_global_device_ids=true | all-gather | bytes 540672 | tf_op jit(solution)/shard_map/while/body/eval_jaxpr/all_gather | solution.py:50
  1536.6 65.9 %all_gather.12 = bf16[16,16384]{1,0:T(8,128)(2,1)S(1)} all-gather(bf16[16,512]{1,0:T(8,128)(2,1)S(1)} %copy_bitcast_fusion.6), channel_id=1, replica_groups=mesh['lag'=4,'row'=32] {'row'}, dimensions={1}, use_global_device_ids=true | all-gather | bytes 540672 | tf_op jit(solution)/shard_map/while/body/eval_jaxpr/all_gather | solution.py:50
  1628.4 31.0 %psum.16 = f32[16,512]{1,0:T(8,128)S(1)} all-reduce(f32[16,512]{1,0:T(8,128)S(1)} %bitcast.81), channel_id=1, replica_groups=mesh['lag'=4,'row'=32] {'lag'}, use_global_device_ids=true, to_apply=%region_1.1 | all-reduce | flops 8192 | bytes 65536 | tf_op jit(solution)/shard_map/while/body/eval_jaxpr/psum | solution.py:45
  1661.0 64.5 %all_gather.12 = bf16[16,16384]{1,0:T(8,128)(2,1)S(1)} all-gather(bf16[16,512]{1,0:T(8,128)(2,1)S(1)} %copy_bitcast_fusion.6), channel_id=1, replica_groups=mesh['lag'=4,'row'=32] {'row'}, dimensions={1}, use_global_device_ids=true | all-gather | bytes 540672 | tf_op jit(solution)/shard_map/while/body/eval_jaxpr/all_gather | solution.py:50
  1783.8 65.9 %all_gather.12 = bf16[16,16384]{1,0:T(8,128)(2,1)S(1)} all-gather(bf16[16,512]{1,0:T(8,128)(2,1)S(1)} %copy_bitcast_fusion.6), channel_id=1, replica_groups=mesh['lag'=4,'row'=32] {'row'}, dimensions={1}, use_global_device_ids=true | all-gather | bytes 540672 | tf_op jit(solution)/shard_map/while/body/eval_jaxpr/all_gather | solution.py:50
  1875.6 31.0 %psum.16 = f32[16,512]{1,0:T(8,128)S(1)} all-reduce(f32[16,512]{1,0:T(8,128)S(1)} %bitcast.81), channel_id=1, replica_groups=mesh['lag'=4,'row'=32] {'lag'}, use_global_device_ids=true, to_apply=%region_1.1 | all-reduce | flops 8192 | bytes 65536 | tf_op jit(solution)/shard_map/while/body/eval_jaxpr/psum | solution.py:45
  1908.2 64.5 %all_gather.12 = bf16[16,16384]{1,0:T(8,128)(2,1)S(1)} all-gather(bf16[16,512]{1,0:T(8,128)(2,1)S(1)} %copy_bitcast_fusion.6), channel_id=1, replica_groups=mesh['lag'=4,'row'=32] {'row'}, dimensions={1}, use_global_device_ids=true | all-gather | bytes 540672 | tf_op jit(solution)/shard_map/while/body/eval_jaxpr/all_gather | solution.py:50
  (291 shorter events, 707.7 us)
Async XLA Ops:
  0.0 7.5 copy-start.1
  0.0 7.6 copy-start.2
  0.0 7.7 copy-start
  8.8 110.6 %collective-permute-start = (bf16[16,16384]{1,0:T(8,128)(2,1)S(1)}, bf16[16,16384]{1,0:T(8,128)(2,1)S(1)}, u32[]{:S(2)}, u32[]{:S(2)}) collective-permute-start(bf16[16,16384]{1,0:T(8,128)(2,1)S(1)} %dynamic-slice_bitcast_fusion.2), channel_id=1, source_target_pairs={{0,32},{32,64},{64,96},{1,33},{33,65},{65,97},{2,34},{34,66},{66,9... | collective-permute-start | bytes 1572872 | tf_op jit(solution)/shard_map/while/body/eval_jaxpr/ppermute | solution.py:10
  121.4 120.7 %collective-permute-start = (bf16[16,16384]{1,0:T(8,128)(2,1)S(1)}, bf16[16,16384]{1,0:T(8,128)(2,1)S(1)}, u32[]{:S(2)}, u32[]{:S(2)}) collective-permute-start(bf16[16,16384]{1,0:T(8,128)(2,1)S(1)} %dynamic-slice_bitcast_fusion.2), channel_id=1, source_target_pairs={{0,32},{32,64},{64,96},{1,33},{33,65},{65,97},{2,34},{34,66},{66,9... | collective-permute-start | bytes 1572872 | tf_op jit(solution)/shard_map/while/body/eval_jaxpr/ppermute | solution.py:10
  244.1 122.3 %collective-permute-start = (bf16[16,16384]{1,0:T(8,128)(2,1)S(1)}, bf16[16,16384]{1,0:T(8,128)(2,1)S(1)}, u32[]{:S(2)}, u32[]{:S(2)}) collective-permute-start(bf16[16,16384]{1,0:T(8,128)(2,1)S(1)} %dynamic-slice_bitcast_fusion.2), channel_id=1, source_target_pairs={{0,32},{32,64},{64,96},{1,33},{33,65},{65,97},{2,34},{34,66},{66,9... | collective-permute-start | bytes 1572872 | tf_op jit(solution)/shard_map/while/body/eval_jaxpr/ppermute | solution.py:10
  368.4 120.9 %collective-permute-start = (bf16[16,16384]{1,0:T(8,128)(2,1)S(1)}, bf16[16,16384]{1,0:T(8,128)(2,1)S(1)}, u32[]{:S(2)}, u32[]{:S(2)}) collective-permute-start(bf16[16,16384]{1,0:T(8,128)(2,1)S(1)} %dynamic-slice_bitcast_fusion.2), channel_id=1, source_target_pairs={{0,32},{32,64},{64,96},{1,33},{33,65},{65,97},{2,34},{34,66},{66,9... | collective-permute-start | bytes 1572872 | tf_op jit(solution)/shard_map/while/body/eval_jaxpr/ppermute | solution.py:10
  491.4 122.3 %collective-permute-start = (bf16[16,16384]{1,0:T(8,128)(2,1)S(1)}, bf16[16,16384]{1,0:T(8,128)(2,1)S(1)}, u32[]{:S(2)}, u32[]{:S(2)}) collective-permute-start(bf16[16,16384]{1,0:T(8,128)(2,1)S(1)} %dynamic-slice_bitcast_fusion.2), channel_id=1, source_target_pairs={{0,32},{32,64},{64,96},{1,33},{33,65},{65,97},{2,34},{34,66},{66,9... | collective-permute-start | bytes 1572872 | tf_op jit(solution)/shard_map/while/body/eval_jaxpr/ppermute | solution.py:10
  615.6 120.9 %collective-permute-start = (bf16[16,16384]{1,0:T(8,128)(2,1)S(1)}, bf16[16,16384]{1,0:T(8,128)(2,1)S(1)}, u32[]{:S(2)}, u32[]{:S(2)}) collective-permute-start(bf16[16,16384]{1,0:T(8,128)(2,1)S(1)} %dynamic-slice_bitcast_fusion.2), channel_id=1, source_target_pairs={{0,32},{32,64},{64,96},{1,33},{33,65},{65,97},{2,34},{34,66},{66,9... | collective-permute-start | bytes 1572872 | tf_op jit(solution)/shard_map/while/body/eval_jaxpr/ppermute | solution.py:10
  738.6 122.2 %collective-permute-start = (bf16[16,16384]{1,0:T(8,128)(2,1)S(1)}, bf16[16,16384]{1,0:T(8,128)(2,1)S(1)}, u32[]{:S(2)}, u32[]{:S(2)}) collective-permute-start(bf16[16,16384]{1,0:T(8,128)(2,1)S(1)} %dynamic-slice_bitcast_fusion.2), channel_id=1, source_target_pairs={{0,32},{32,64},{64,96},{1,33},{33,65},{65,97},{2,34},{34,66},{66,9... | collective-permute-start | bytes 1572872 | tf_op jit(solution)/shard_map/while/body/eval_jaxpr/ppermute | solution.py:10
  862.8 121.0 %collective-permute-start = (bf16[16,16384]{1,0:T(8,128)(2,1)S(1)}, bf16[16,16384]{1,0:T(8,128)(2,1)S(1)}, u32[]{:S(2)}, u32[]{:S(2)}) collective-permute-start(bf16[16,16384]{1,0:T(8,128)(2,1)S(1)} %dynamic-slice_bitcast_fusion.2), channel_id=1, source_target_pairs={{0,32},{32,64},{64,96},{1,33},{33,65},{65,97},{2,34},{34,66},{66,9... | collective-permute-start | bytes 1572872 | tf_op jit(solution)/shard_map/while/body/eval_jaxpr/ppermute | solution.py:10
  985.8 122.2 %collective-permute-start = (bf16[16,16384]{1,0:T(8,128)(2,1)S(1)}, bf16[16,16384]{1,0:T(8,128)(2,1)S(1)}, u32[]{:S(2)}, u32[]{:S(2)}) collective-permute-start(bf16[16,16384]{1,0:T(8,128)(2,1)S(1)} %dynamic-slice_bitcast_fusion.2), channel_id=1, source_target_pairs={{0,32},{32,64},{64,96},{1,33},{33,65},{65,97},{2,34},{34,66},{66,9... | collective-permute-start | bytes 1572872 | tf_op jit(solution)/shard_map/while/body/eval_jaxpr/ppermute | solution.py:10
  1110.0 121.0 %collective-permute-start = (bf16[16,16384]{1,0:T(8,128)(2,1)S(1)}, bf16[16,16384]{1,0:T(8,128)(2,1)S(1)}, u32[]{:S(2)}, u32[]{:S(2)}) collective-permute-start(bf16[16,16384]{1,0:T(8,128)(2,1)S(1)} %dynamic-slice_bitcast_fusion.2), channel_id=1, source_target_pairs={{0,32},{32,64},{64,96},{1,33},{33,65},{65,97},{2,34},{34,66},{66,9... | collective-permute-start | bytes 1572872 | tf_op jit(solution)/shard_map/while/body/eval_jaxpr/ppermute | solution.py:10
  1233.1 122.2 %collective-permute-start = (bf16[16,16384]{1,0:T(8,128)(2,1)S(1)}, bf16[16,16384]{1,0:T(8,128)(2,1)S(1)}, u32[]{:S(2)}, u32[]{:S(2)}) collective-permute-start(bf16[16,16384]{1,0:T(8,128)(2,1)S(1)} %dynamic-slice_bitcast_fusion.2), channel_id=1, source_target_pairs={{0,32},{32,64},{64,96},{1,33},{33,65},{65,97},{2,34},{34,66},{66,9... | collective-permute-start | bytes 1572872 | tf_op jit(solution)/shard_map/while/body/eval_jaxpr/ppermute | solution.py:10
  1357.3 121.0 %collective-permute-start = (bf16[16,16384]{1,0:T(8,128)(2,1)S(1)}, bf16[16,16384]{1,0:T(8,128)(2,1)S(1)}, u32[]{:S(2)}, u32[]{:S(2)}) collective-permute-start(bf16[16,16384]{1,0:T(8,128)(2,1)S(1)} %dynamic-slice_bitcast_fusion.2), channel_id=1, source_target_pairs={{0,32},{32,64},{64,96},{1,33},{33,65},{65,97},{2,34},{34,66},{66,9... | collective-permute-start | bytes 1572872 | tf_op jit(solution)/shard_map/while/body/eval_jaxpr/ppermute | solution.py:10
  1480.3 122.2 %collective-permute-start = (bf16[16,16384]{1,0:T(8,128)(2,1)S(1)}, bf16[16,16384]{1,0:T(8,128)(2,1)S(1)}, u32[]{:S(2)}, u32[]{:S(2)}) collective-permute-start(bf16[16,16384]{1,0:T(8,128)(2,1)S(1)} %dynamic-slice_bitcast_fusion.2), channel_id=1, source_target_pairs={{0,32},{32,64},{64,96},{1,33},{33,65},{65,97},{2,34},{34,66},{66,9... | collective-permute-start | bytes 1572872 | tf_op jit(solution)/shard_map/while/body/eval_jaxpr/ppermute | solution.py:10
  1604.5 121.0 %collective-permute-start = (bf16[16,16384]{1,0:T(8,128)(2,1)S(1)}, bf16[16,16384]{1,0:T(8,128)(2,1)S(1)}, u32[]{:S(2)}, u32[]{:S(2)}) collective-permute-start(bf16[16,16384]{1,0:T(8,128)(2,1)S(1)} %dynamic-slice_bitcast_fusion.2), channel_id=1, source_target_pairs={{0,32},{32,64},{64,96},{1,33},{33,65},{65,97},{2,34},{34,66},{66,9... | collective-permute-start | bytes 1572872 | tf_op jit(solution)/shard_map/while/body/eval_jaxpr/ppermute | solution.py:10
  1727.5 122.2 %collective-permute-start = (bf16[16,16384]{1,0:T(8,128)(2,1)S(1)}, bf16[16,16384]{1,0:T(8,128)(2,1)S(1)}, u32[]{:S(2)}, u32[]{:S(2)}) collective-permute-start(bf16[16,16384]{1,0:T(8,128)(2,1)S(1)} %dynamic-slice_bitcast_fusion.2), channel_id=1, source_target_pairs={{0,32},{32,64},{64,96},{1,33},{33,65},{65,97},{2,34},{34,66},{66,9... | collective-permute-start | bytes 1572872 | tf_op jit(solution)/shard_map/while/body/eval_jaxpr/ppermute | solution.py:10
  1851.7 121.0 %collective-permute-start = (bf16[16,16384]{1,0:T(8,128)(2,1)S(1)}, bf16[16,16384]{1,0:T(8,128)(2,1)S(1)}, u32[]{:S(2)}, u32[]{:S(2)}) collective-permute-start(bf16[16,16384]{1,0:T(8,128)(2,1)S(1)} %dynamic-slice_bitcast_fusion.2), channel_id=1, source_target_pairs={{0,32},{32,64},{64,96},{1,33},{33,65},{65,97},{2,34},{34,66},{66,9... | collective-permute-start | bytes 1572872 | tf_op jit(solution)/shard_map/while/body/eval_jaxpr/ppermute | solution.py:10
where the time goes:
time: 1990 us; the launch traced here: 1970 us
  blocking collectives  1530 us (77%)
  local copies, waits for them, and re-layouts  264 us (13%)
  matrix products  144 us (7%)
  starting transfers between devices  20.7 us (1%)
    all_gather x16, blocking collectives, advance(): newest_all = lax.all_gather(solved, 'row', axis=1, tiled=True)  1050 us
    psum x16, blocking collectives, advance(): total = lax.psum(partial_value, 'lag')  478 us
    reshape x16, local copies, waits for them, and re-layouts, advance(): blocks = buffer.reshape(lag_dev, pulses, nblocks, tile)  130 us
    dot_general x16, matrix products, advance(): jnp.einsum('jbkic,jbkpc->pbi', tiles, picked, preferred_element_type=jnp....  129 us
    gather x16, local copies, waits for them, and re-layouts, advance(): picked = blocks[slot_of[:, None, None], :, columns]  96.7 us
  transfers between devices with their start and end apart: 16, of which 0 were waited for; matrix products, arithmetic and copies ran while one was open for 20% of the time, Pallas kernels for 0%

commit v1 on v0

v1 whole, which is shorter than its diff:
```python
import jax
import jax.numpy as jnp
from jax import lax
from jax.experimental import pallas as pl
from jax.experimental.pallas import tpu as pltpu
from jax.sharding import PartitionSpec as P

MESH = pl.DeviceIdType.MESH
LAG_AXIS, ROW_AXIS = "lag", "row"
NY, NZ, NX = 2, 4, 4
ROWS = NY * NZ * NX
GROUPS = 4
LAGS = 16
RB = 4
KS = 8
T = 128
PULSES = 16
HALF = 8
STEPS = 16
SENT = STEPS - 1
NB = 128
WIDTH = RB * T
NEAR = 8


def ring_hops(d, n):
    return min(d, n - d)


OFFSETS = sorted(
    [(a, b, c) for a in range(NY) for b in range(NZ) for c in range(NX)][1:],
    key=lambda o: -(o[0] + ring_hops(o[1], NZ) + ring_hops(o[2], NX)),
)


def dot_t(a, b):
    return lax.dot_general(a, b, (((1,), (1,)), ((), ())), preferred_element_type=jnp.float32)


def kernel(
    columns, counts, hist_hbm, tiles_hbm, inv_hbm, exc_hbm, out_ref,
    tiles, h0, land, work, inv, exc, acc, base, part, parts, solf, outbuf,
    tsem, hsem, isem, esem, recv_a, recv_b, send_a, send_b,
    hrecv, slice_recv, slice_send, fwd_send, stream_send, part_send, part_recv, out_send, out_recv,
):
    g = lax.axis_index(LAG_AXIS)
    r = lax.axis_index(ROW_AXIS)
    y, z, x = r // (NZ * NX), (r // NX) % NZ, r % NX
    partner = (NY - 1 - y) * (NZ * NX) + z * NX + x

    def peer(o):
        return ((y + o[0]) % NY) * (NZ * NX) + ((z + o[1]) % NZ) * NX + (x + o[2]) % NX

    for l in range(LAGS):
        pltpu.make_async_copy(tiles_hbm.at[l], tiles.at[l], tsem.at[l]).start()

    def load_block(c, carry):
        pltpu.make_async_copy(
            hist_hbm.at[:, :, pl.ds(pl.multiple_of(c * T, T), T)], h0.at[:, c], hsem
        ).start()
        return carry

    lax.fori_loop(0, NB, load_block, 0)
    inv_copy = pltpu.make_async_copy(inv_hbm, inv, isem)
    inv_copy.start()
    exc_copy = pltpu.make_async_copy(exc_hbm, exc, esem)
    exc_copy.start()

    barrier = pltpu.get_barrier_semaphore()

    def greet(lag, row):
        pl.semaphore_signal(barrier, inc=1, device_id=(lag, row), device_id_type=MESH)

    @pl.when(g % 2 == 0)
    def _():
        for o in OFFSETS:
            greet(g, peer(o))

    @pl.when(g == 0)
    def _():
        for other in (1, 2, 3):
            greet(other, r)
        pl.semaphore_wait(barrier, ROWS - 1 + 3)

    @pl.when(g == 1)
    def _():
        greet(0, r)
        greet(2, partner)
        pl.semaphore_wait(barrier, 2)

    @pl.when(g == 2)
    def _():
        greet(0, r)
        greet(3, r)
        greet(1, partner)
        pl.semaphore_wait(barrier, ROWS - 1 + 3)

    @pl.when(g == 3)
    def _():
        greet(0, r)
        greet(2, r)
        pl.semaphore_wait(barrier, 2)

    def slice_copy(tau, i):
        c = RB * partner + i
        return pltpu.make_async_remote_copy(
            hist_hbm.at[LAGS - 1 - tau, :, pl.ds(pl.multiple_of(c * T, T), T)],
            land.at[tau, c],
            slice_send.at[tau],
            slice_recv.at[tau],
            device_id=(2, partner),
            device_id_type=MESH,
        )

    @pl.when(g == 1)
    def _():
        def one(tau, carry):
            for i in range(RB):
                slice_copy(tau, i).start()
            return carry

        lax.fori_loop(0, SENT, one, 0)

    zero_block = jnp.zeros((T // 8, T), jnp.bfloat16)
    acc[...] = jnp.zeros_like(acc)
    for e in range(LAGS):
        h0[e, NB] = zero_block
    for tau in range(SENT):
        work[tau, 0, NB] = zero_block
        work[tau, 1, NB] = zero_block

    pltpu.make_async_copy(h0.at[:, pl.ds(0, NB)], h0.at[:, pl.ds(0, NB)], hsem).wait()

    def stream_copy(tau):
        return pltpu.make_async_remote_copy(
            h0.at[LAGS - 1 - tau, pl.ds(0, NB)],
            land.at[tau],
            stream_send.at[tau],
            hrecv.at[tau],
            device_id=(g + 1, r),
            device_id_type=MESH,
        )

    @pl.when(g % 2 == 0)
    def _():
        def one(tau, carry):
            stream_copy(tau).start()
            return carry

        lax.fori_loop(0, SENT, one, 0)

    def column(l, b, k):
        return jnp.where(k < counts[l, b], columns[l, b, k], NB)

    def weights(l, b):
        return jnp.concatenate([tiles[l, b, k] for k in range(KS)], axis=1)

    for quarter in range(4):
        entries = 4 * quarter + 4

        def own_lag(l, carry):
            pltpu.make_async_copy(tiles.at[l], tiles.at[l], tsem.at[l]).wait()
            for b in range(RB):
                xs = [
                    h0[0:entries, column(l, b, k)].reshape(entries * PULSES, T) for k in range(KS)
                ]
                got = dot_t(jnp.concatenate(xs, axis=1), weights(l, b))
                here = (pl.ds(LAGS - 1 - l, entries), slice(None), pl.ds(b * T, T))
                acc[here] += got.reshape(entries, PULSES, T)
            return carry

        lax.fori_loop(4 * quarter, 4 * quarter + 4, own_lag, 0)

    inv_copy.wait()
    exc_copy.wait()

    def part_copy(s, ch):
        return pltpu.make_async_remote_copy(
            part.at[s, ch],
            parts.at[s, ch, g - 1],
            part_send.at[s],
            part_recv.at[s],
            device_id=(0, r),
            device_id_type=MESH,
        )

    def send_part(s):
        for ch in range(2):
            part[s, ch] = acc[STEPS - 1 - s, pl.ds(ch * HALF, HALF), :]
        for ch in range(2):
            part_copy(s, ch).start()

    def forward_copy(tau, o):
        here = land.at[tau, pl.ds(RB * r, RB)]
        return pltpu.make_async_remote_copy(
            here, here, fwd_send.at[tau], hrecv.at[tau], device_id=(2, peer(o)), device_id_type=MESH
        )

    def forward(tau):
        here = land.at[tau, pl.ds(RB * r, RB)]
        pltpu.make_async_copy(here, here, slice_recv.at[tau]).wait()
        for o in OFFSETS:
            forward_copy(tau, o).start()

    @pl.when(g > 0)
    def _():
        send_part(0)

        @pl.when(g == 2)
        def _():
            def one(tau, carry):
                forward(tau)
                return carry

            lax.fori_loop(0, 2, one, 0)

        def entry(tau, carry):
            @pl.when((g == 2) & (tau < SENT - 2))
            def _():
                forward(tau + 2)

            @pl.when(g == 2)
            def _():
                arrived = land.at[tau, pl.ds(0, NB - RB)]
                pltpu.make_async_copy(arrived, arrived, hrecv.at[tau]).wait()

            @pl.when(g != 2)
            def _():
                pltpu.make_async_copy(land.at[tau], land.at[tau], hrecv.at[tau]).wait()

            work[tau, 0, pl.ds(0, NB)] = land[tau]

            def push(lag, carry):
                for b in range(RB):
                    xs = [work[tau, 0, column(lag - 1, b, k)] for k in range(KS)]
                    got = dot_t(jnp.concatenate(xs, axis=1), weights(lag - 1, b))
                    here = (STEPS - 1 - (tau + lag), slice(None), pl.ds(b * T, T))
                    acc[here] += got
                return carry

            lax.fori_loop(1, STEPS - tau, push, 0)
            send_part(tau + 1)
            return carry

        lax.fori_loop(0, SENT, entry, 0)

    low = lax.broadcasted_iota(jnp.int32, (2 * HALF, T), 0) < HALF
    keep_low = jnp.where(low, 1.0, 0.0).astype(jnp.bfloat16)
    keep_high = jnp.where(low, 0.0, 1.0).astype(jnp.bfloat16)
    recv = (recv_a, recv_b)
    send = (send_a, send_b)

    def own_slot(s, ch):
        return land.at[s, pl.ds(ch * (NB // 2) + 2 * r, 2)]

    def solution_copy(s, ch, o):
        here = own_slot(s, ch)
        return pltpu.make_async_remote_copy(
            here, here, send[ch].at[s], recv[ch].at[s], device_id=(0, peer(o)), device_id_type=MESH
        )

    def out_copy(s, other):
        return pltpu.make_async_remote_copy(
            outbuf.at[s], outbuf.at[s], out_send.at[s], out_recv, device_id=(other, r), device_id_type=MESH
        )

    def folded(got):
        return got[0:HALF] + got[HALF : 2 * HALF]

    def set_base(s):
        pltpu.make_async_copy(parts.at[s], parts.at[s], part_recv.at[s]).wait()
        for ch in range(2):
            rows = pl.ds(ch * HALF, HALF)
            other = parts[s, ch, 0] + parts[s, ch, 1] + parts[s, ch, 2]
            base[ch] = exc[s, rows, :] - (acc[STEPS - 1 - s, rows, :] + other)

    def chain(s, ch, first):
        if not first:
            tau = s - 1
            arrived = land.at[tau, pl.ds(0, NB // 2 - 2)]
            pltpu.make_async_copy(arrived, arrived, recv[ch].at[tau]).wait()
            pairs = land[tau, pl.ds(ch * (NB // 2), NB // 2)]
            split = jnp.stack([pairs * keep_low, pairs * keep_high], axis=1)
            work[tau, ch, pl.ds(0, NB)] = split.reshape(NB, 2 * HALF, T)
        solved = []
        for b in range(RB):
            cols = pl.ds(b * T, T)
            field = base[ch, :, cols]
            if not first:
                xs = [work[tau, ch, column(0, b, k)] for k in range(KS)]
                field = field - folded(dot_t(jnp.concatenate(xs, axis=1), weights(0, b)))
            solved.append(dot_t(field.astype(jnp.bfloat16), inv[b]))
        for b in range(RB):
            solf[pl.ds(ch * HALF, HALF), pl.ds(b * T, T)] = solved[b]

        def publish():
            for i in range(2):
                pair = jnp.concatenate([solved[2 * i], solved[2 * i + 1]], axis=0)
                land[s, ch * (NB // 2) + 2 * r + i] = pair.astype(jnp.bfloat16)
            for o in OFFSETS:
                solution_copy(s, ch, o).start()

        if first:
            publish()
        else:
            pl.when(s < SENT)(publish)

    def hand_out(s):
        outbuf[s] = solf[...].astype(jnp.bfloat16)
        for other in (1, 2, 3):
            out_copy(s, other).start()

    def later(s):
        near = jnp.minimum(s, NEAR - 1)
        far = jnp.maximum(NEAR - s, 0)

        def one(n, carry):
            is_near = n < near
            lag = jnp.where(is_near, n + 2, n - near + NEAR + 1)
            tau = jnp.where(is_near, s + 1 - lag, s - 1)
            target = tau + lag
            for b in range(RB):
                cs = [column(lag - 1, b, k) for k in range(KS)]
                xa = jnp.concatenate([work[tau, 0, c] for c in cs], axis=1)
                xb = jnp.concatenate([work[tau, 1, c] for c in cs], axis=1)
                got = dot_t(jnp.concatenate([xa, xb], axis=0), weights(lag - 1, b))
                here = (STEPS - 1 - target, slice(None), pl.ds(b * T, T))
                acc[here] += jnp.concatenate(
                    [folded(got[0 : 2 * HALF]), folded(got[2 * HALF : 4 * HALF])], axis=0
                )
            return carry

        lax.fori_loop(0, near + far, one, 0)

    @pl.when(g == 0)
    def _():
        set_base(0)
        chain(0, 0, True)
        chain(0, 1, True)
        hand_out(0)
        set_base(1)

        def step(s, carry):
            chain(s, 0, False)
            chain(s, 1, False)
            hand_out(s)

            @pl.when(s < STEPS - 1)
            def _():
                later(s)
                set_base(s + 1)

            return carry

        lax.fori_loop(1, STEPS, step, 0)

        def drain(s, carry):
            sent = land.at[s, pl.ds(0, NB // 2 - 2)]
            for ch in range(2):
                pltpu.make_async_copy(sent, sent, send[ch].at[s]).wait()
            return carry

        lax.fori_loop(0, SENT, drain, 0)

        def drain_out(s, carry):
            for other in (1, 2, 3):
                out_copy(s, other).wait_send()
            return carry

        lax.fori_loop(0, STEPS, drain_out, 0)

    @pl.when(g > 0)
    def _():
        pltpu.make_async_copy(outbuf, outbuf, out_recv).wait()

        def drain(s, carry):
            pltpu.make_async_copy(part.at[s], part.at[s], part_send.at[s]).wait()
            return carry

        lax.fori_loop(0, STEPS, drain, 0)

    @pl.when(g % 2 == 0)
    def _():
        def drain(tau, carry):
            stream_copy(tau).wait_send()
            return carry

        lax.fori_loop(0, SENT, drain, 0)

    @pl.when(g == 1)
    def _():
        def drain(tau, carry):
            sent = land.at[tau, pl.ds(0, RB)]
            pltpu.make_async_copy(sent, sent, slice_send.at[tau]).wait()
            return carry

        lax.fori_loop(0, SENT, drain, 0)

    @pl.when(g == 2)
    def _():
        def drain(tau, carry):
            sent = land.at[tau, pl.ds(0, NB - RB)]
            pltpu.make_async_copy(sent, sent, fwd_send.at[tau]).wait()
            return carry

        lax.fori_loop(0, SENT, drain, 0)

    out_ref[...] = outbuf[...]


def local(history, tiles, columns, counts, inverse, excitation):
    smem = pl.BlockSpec(memory_space=pltpu.SMEM)
    hbm = pl.BlockSpec(memory_space=pl.ANY)
    dma = pltpu.SemaphoreType.DMA
    bf16, f32 = jnp.bfloat16, jnp.float32
    return pl.pallas_call(
        kernel,
        out_shape=jax.ShapeDtypeStruct((STEPS, PULSES, WIDTH), bf16),
        in_specs=[smem, smem, hbm, hbm, hbm, hbm],
        out_specs=pl.BlockSpec(memory_space=pltpu.VMEM),
        scratch_shapes=[
            pltpu.VMEM((LAGS, RB, KS, T, T), bf16),
            pltpu.VMEM((LAGS, NB + 1, PULSES, T), bf16),
            pltpu.VMEM((SENT, NB, PULSES, T), bf16),
            pltpu.VMEM((SENT, 2, NB + 1, PULSES, T), bf16),
            pltpu.VMEM((RB, T, T), bf16),
            pltpu.VMEM((STEPS, PULSES, WIDTH), f32),
            pltpu.VMEM((STEPS + 3, PULSES, WIDTH), f32),
            pltpu.VMEM((2, HALF, WIDTH), f32),
            pltpu.VMEM((STEPS, 2, HALF, WIDTH), f32),
            pltpu.VMEM((STEPS, 2, 3, HALF, WIDTH), f32),
            pltpu.VMEM((PULSES, WIDTH), f32),
            pltpu.VMEM((STEPS, PULSES, WIDTH), bf16),
            dma((LAGS,)), dma, dma, dma,
            dma((SENT,)), dma((SENT,)), dma((SENT,)), dma((SENT,)),
            dma((SENT,)), dma((SENT,)), dma((SENT,)), dma((SENT,)), dma((SENT,)),
            dma((STEPS,)), dma((STEPS,)), dma((STEPS,)), dma,
        ],
        compiler_params=pltpu.CompilerParams(
            collective_id=0, has_side_effects=True, vmem_limit_bytes=60 << 20
        ),
    )(columns, counts, history, tiles, inverse, excitation)


def solution(mesh):
    return jax.shard_map(
        local,
        mesh=mesh,
        in_specs=(
            P("lag", None, None),
            P("lag", "row", None, None, None),
            P("lag", "row", None),
            P("lag", "row"),
            P("row", None, None),
            P(None, None, "row"),
        ),
        out_specs=P(None, None, "row"),
        check_vma=False,
    )
```

time: 1990 us -> 147 us (0.07)
  blocking collectives: 1530 us -> 0 us
  local copies, waits for them, and re-layouts: 264 us -> 4.42 us
  matrix products: 144 us -> 0 us
  Pallas kernels: 0 us -> 143 us
  starting transfers between devices: 20.7 us -> 0 us
    all_gather x16 -> x0, blocking collectives: 1050 us -> none  [advance(): newest_all = lax.all_gather(solved, 'row', axis=1, tiled=True)]
    psum x16 -> x0, blocking collectives: 478 us -> none  [advance(): total = lax.psum(partial_value, 'lag')]
    dot_general x32 -> x0, matrix products: 144 us -> none  [the longest x16 129 us: advance(): jnp.einsum('jbkic,jbkpc->pbi', tiles, picked, preferred_element_type=jnp....]
    pallas_call x0 -> x1, Pallas kernels: none -> 143 us  [local(): pl.pallas_call(kernel, out_shape=jax.ShapeDtypeStruct((STEPS, PULSES, WID...]
    reshape x48 -> x0, local copies, waits for them, and re-layouts: 130 us -> none  [the longest x16 130 us: advance(): blocks = buffer.reshape(lag_dev, pulses, nblocks, tile)]
    gather x16 -> x0, local copies, waits for them, and re-layouts: 96.7 us -> none  [advance(): picked = blocks[slot_of[:, None, None], :, columns]]
    ppermute x16 -> x0, starting transfers between devices: 20.7 us -> none  [passed_along(): return lax.ppermute(block, axis, route)]
  transfers between devices with their start and end apart: 16 -> 0, of which waited for: 0 -> 0; matrix products, arithmetic and copies ran while one was open for 20% -> 0% of each run, Pallas kernels for 0% -> 0%
where the time goes in v1:
time: 147 us
  Pallas kernels  143 us (97%)
  local copies, waits for them, and re-layouts  4.42 us (3%)
    pallas_call x1, Pallas kernels, local(): pl.pallas_call(kernel, out_shape=jax.ShapeDtypeStruct((STEPS, PULSES, WID...  143 us
    unnamed x3, local copies, waits for them, and re-layouts  4.42 us

profile of v1, /device:TPU:25, one launch (start us, length us, event | category | flops | bytes accessed | tf_op | source)
XLA Modules:
  0.0 147.0 jit_solution(9786978177793419488)
XLA Ops:
  0.0 1.3 copy.8.counts
  1.3 1.4 copy.7.columns
  2.8 142.6 %shard_map.64 = bf16[16,16,512]{2,1,0:T(8,128)(2,1)} custom-call(s32[16,4,8]{2,1,0:T(4,128)} %copy.7.columns, s32[16,4]{1,0:T(8,128)} %copy.8.counts, bf16[16,16,16384]{2,1,0:T(8,128)(2,1)} %hist_hbm.1, bf16[16,4,8,128,128]{4,3,2,1,0:T(8,128)(2,1)} %tiles_hbm.1, bf16[4,128,128]{2,1,0:T(8,128)(2,1)} %inv_hbm.1, f32[16,16,512]{2,1,0:T(8,128)} %exc_hbm.1), custom_call_target="tpu_custom_call" | custom-call | tf_op jit(solution)/shard_map/pallas_call | solution.py:416
  145.3 1.7 %copy.10 = bf16[16,16,512]{2,1,0:T(8,128)(2,1)} copy(bf16[16,16,512]{2,1,0:T(8,128)(2,1)} %shard_map.64) | data formatting | bytes 524288

commit v2 on v1

--- a/solution.py
+++ b/solution.py
@@ -39,7 +39,7 @@
 
 def kernel(
     columns, counts, hist_hbm, tiles_hbm, inv_hbm, exc_hbm, out_ref,
-    tiles, h0, land, work, inv, exc, acc, base, part, parts, solf, outbuf,
+    tiles, h0, land, work, inv, exc, acc, base, first_lag, part, parts, solf, outbuf,
     tsem, hsem, isem, esem, recv_a, recv_b, send_a, send_b,
     hrecv, slice_recv, slice_send, fwd_send, stream_send, part_send, part_recv, out_send, out_recv,
 ):
@@ -51,8 +51,45 @@
     def peer(o):
         return ((y + o[0]) % NY) * (NZ * NX) + ((z + o[1]) % NZ) * NX + (x + o[2]) % NX
 
-    for l in range(LAGS):
-        pltpu.make_async_copy(tiles_hbm.at[l], tiles.at[l], tsem.at[l]).start()
+    barrier = pltpu.get_barrier_semaphore()
+
+    def greet(lag, row):
+        pl.semaphore_signal(barrier, inc=1, device_id=(lag, row), device_id_type=MESH)
+
+    @pl.when(g % 2 == 0)
+    def _():
+        for o in OFFSETS:
+            greet(g, peer(o))
+
+    @pl.when(g == 0)
+    def _():
+        for other in (1, 2, 3):
+            greet(other, r)
+
+    @pl.when(g == 1)
+    def _():
+        greet(0, r)
+        greet(2, partner)
+
+    @pl.when(g == 2)
+    def _():
+        greet(0, r)
+        greet(3, r)
+        greet(1, partner)
+
+    @pl.when(g == 3)
+    def _():
+        greet(0, r)
+        greet(2, r)
+
+    def wait_for_greetings():
+        @pl.when(g % 2 == 0)
+        def _():
+            pl.semaphore_wait(barrier, ROWS - 1 + 3)
+
+        @pl.when(g % 2 == 1)
+        def _():
+            pl.semaphore_wait(barrier, 2)
 
     def load_block(c, carry):
         pltpu.make_async_copy(
@@ -61,65 +98,12 @@
         return carry
 
     lax.fori_loop(0, NB, load_block, 0)
+    for l in range(LAGS):
+        pltpu.make_async_copy(tiles_hbm.at[l], tiles.at[l], tsem.at[l]).start()
     inv_copy = pltpu.make_async_copy(inv_hbm, inv, isem)
     inv_copy.start()
     exc_copy = pltpu.make_async_copy(exc_hbm, exc, esem)
     exc_copy.start()
-
-    barrier = pltpu.get_barrier_semaphore()
-
-    def greet(lag, row):
-        pl.semaphore_signal(barrier, inc=1, device_id=(lag, row), device_id_type=MESH)
-
-    @pl.when(g % 2 == 0)
-    def _():
-        for o in OFFSETS:
-            greet(g, peer(o))
-
-    @pl.when(g == 0)
-    def _():
-        for other in (1, 2, 3):
-            greet(other, r)
-        pl.semaphore_wait(barrier, ROWS - 1 + 3)
-
-    @pl.when(g == 1)
-    def _():
-        greet(0, r)
-        greet(2, partner)
-        pl.semaphore_wait(barrier, 2)
-
-    @pl.when(g == 2)
-    def _():
-        greet(0, r)
-        greet(3, r)
-        greet(1, partner)
-        pl.semaphore_wait(barrier, ROWS - 1 + 3)
-
-    @pl.when(g == 3)
-    def _():
-        greet(0, r)
-        greet(2, r)
-        pl.semaphore_wait(barrier, 2)
-
-    def slice_copy(tau, i):
-        c = RB * partner + i
-        return pltpu.make_async_remote_copy(
-            hist_hbm.at[LAGS - 1 - tau, :, pl.ds(pl.multiple_of(c * T, T), T)],
-            land.at[tau, c],
-            slice_send.at[tau],
-            slice_recv.at[tau],
-            device_id=(2, partner),
-            device_id_type=MESH,
-        )
-
-    @pl.when(g == 1)
-    def _():
-        def one(tau, carry):
-            for i in range(RB):
-                slice_copy(tau, i).start()
-            return carry
-
-        lax.fori_loop(0, SENT, one, 0)
 
     zero_block = jnp.zeros((T // 8, T), jnp.bfloat16)
     acc[...] = jnp.zeros_like(acc)
@@ -131,6 +115,17 @@
 
     pltpu.make_async_copy(h0.at[:, pl.ds(0, NB)], h0.at[:, pl.ds(0, NB)], hsem).wait()
 
+    def slice_copy(tau):
+        cs = pl.ds(RB * partner, RB)
+        return pltpu.make_async_remote_copy(
+            h0.at[LAGS - 1 - tau, cs],
+            land.at[tau, cs],
+            slice_send.at[tau],
+            slice_recv.at[tau],
+            device_id=(2, partner),
+            device_id_type=MESH,
+        )
+
     def stream_copy(tau):
         return pltpu.make_async_remote_copy(
             h0.at[LAGS - 1 - tau, pl.ds(0, NB)],
@@ -141,16 +136,37 @@
             device_id_type=MESH,
         )
 
-    @pl.when(g % 2 == 0)
-    def _():
-        def one(tau, carry):
-            stream_copy(tau).start()
-            return carry
-
-        lax.fori_loop(0, SENT, one, 0)
+    def send_history():
+        @pl.when(g == 1)
+        def _():
+            def one(tau, carry):
+                slice_copy(tau).start()
+                return carry
+
+            lax.fori_loop(0, SENT, one, 0)
+
+        @pl.when(g % 2 == 0)
+        def _():
+            def one(tau, carry):
+                stream_copy(tau).start()
+                return carry
+
+            lax.fori_loop(0, SENT, one, 0)
+
+    def forward_copy(tau, o):
+        here = land.at[tau, pl.ds(RB * r, RB)]
+        return pltpu.make_async_remote_copy(
+            here, here, fwd_send.at[tau], hrecv.at[tau], device_id=(2, peer(o)), device_id_type=MESH
+        )
+
+    def forward(tau):
+        here = land.at[tau, pl.ds(RB * r, RB)]
+        pltpu.make_async_copy(here, here, slice_recv.at[tau]).wait()
+        for o in OFFSETS:
+            forward_copy(tau, o).start()
 
     def column(l, b, k):
-        return jnp.where(k < counts[l, b], columns[l, b, k], NB)
+        return jnp.where(k < counts[b, l], columns[b, k, l], NB)
 
     def weights(l, b):
         return jnp.concatenate([tiles[l, b, k] for k in range(KS)], axis=1)
@@ -170,6 +186,15 @@
             return carry
 
         lax.fori_loop(4 * quarter, 4 * quarter + 4, own_lag, 0)
+        if quarter == 0:
+            wait_for_greetings()
+            send_history()
+        if quarter == 2:
+
+            @pl.when(g == 2)
+            def _():
+                forward(0)
+
 
     inv_copy.wait()
     exc_copy.wait()
@@ -190,34 +215,14 @@
         for ch in range(2):
             part_copy(s, ch).start()
 
-    def forward_copy(tau, o):
-        here = land.at[tau, pl.ds(RB * r, RB)]
-        return pltpu.make_async_remote_copy(
-            here, here, fwd_send.at[tau], hrecv.at[tau], device_id=(2, peer(o)), device_id_type=MESH
-        )
-
-    def forward(tau):
-        here = land.at[tau, pl.ds(RB * r, RB)]
-        pltpu.make_async_copy(here, here, slice_recv.at[tau]).wait()
-        for o in OFFSETS:
-            forward_copy(tau, o).start()
-
     @pl.when(g > 0)
     def _():
         send_part(0)
 
-        @pl.when(g == 2)
-        def _():
-            def one(tau, carry):
-                forward(tau)
-                return carry
-
-            lax.fori_loop(0, 2, one, 0)
-
         def entry(tau, carry):
-            @pl.when((g == 2) & (tau < SENT - 2))
+            @pl.when((g == 2) & (tau < SENT - 1))
             def _():
-                forward(tau + 2)
+                forward(tau + 1)
 
             @pl.when(g == 2)
             def _():
@@ -238,8 +243,9 @@
                     acc[here] += got
                 return carry
 
-            lax.fori_loop(1, STEPS - tau, push, 0)
+            push(1, 0)
             send_part(tau + 1)
+            lax.fori_loop(2, STEPS - tau, push, 0)
             return carry
 
         lax.fori_loop(0, SENT, entry, 0)
@@ -269,10 +275,11 @@
 
     def set_base(s):
         pltpu.make_async_copy(parts.at[s], parts.at[s], part_recv.at[s]).wait()
-        for ch in range(2):
-            rows = pl.ds(ch * HALF, HALF)
-            other = parts[s, ch, 0] + parts[s, ch, 1] + parts[s, ch, 2]
-            base[ch] = exc[s, rows, :] - (acc[STEPS - 1 - s, rows, :] + other)
+        other = [parts[s, ch, 0] + parts[s, ch, 1] + parts[s, ch, 2] for ch in range(2)]
+        field = exc[s] - (acc[STEPS - 1 - s] + jnp.concatenate(other, axis=0))
+        rhs = field.astype(jnp.bfloat16)
+        for b in range(RB):
+            base[:, pl.ds(b * T, T)] = dot_t(rhs[:, b * T : (b + 1) * T], inv[b])
 
     def chain(s, ch, first):
         if not first:
@@ -285,11 +292,14 @@
         solved = []
         for b in range(RB):
             cols = pl.ds(b * T, T)
-            field = base[ch, :, cols]
+            value = base[pl.ds(ch * HALF, HALF), cols]
             if not first:
                 xs = [work[tau, ch, column(0, b, k)] for k in range(KS)]
-                field = field - folded(dot_t(jnp.concatenate(xs, axis=1), weights(0, b)))
-            solved.append(dot_t(field.astype(jnp.bfloat16), inv[b]))
+                got = jnp.dot(
+                    jnp.concatenate(xs, axis=1), first_lag[b], preferred_element_type=jnp.float32
+                )
+                value = value - folded(got)
+            solved.append(value)
         for b in range(RB):
             solf[pl.ds(ch * HALF, HALF), pl.ds(b * T, T)] = solved[b]
 
@@ -334,6 +344,12 @@
 
     @pl.when(g == 0)
     def _():
+        for b in range(RB):
+            for k in range(KS):
+                product = lax.dot_general(
+                    tiles[0, b, k], inv[b], (((0,), (1,)), ((), ())), preferred_element_type=jnp.float32
+                )
+                first_lag[b, pl.ds(k * T, T), :] = product.astype(jnp.bfloat16)
         set_base(0)
         chain(0, 0, True)
         chain(0, 1, True)
@@ -426,7 +442,8 @@
             pltpu.VMEM((RB, T, T), bf16),
             pltpu.VMEM((STEPS, PULSES, WIDTH), f32),
             pltpu.VMEM((STEPS + 3, PULSES, WIDTH), f32),
-            pltpu.VMEM((2, HALF, WIDTH), f32),
+            pltpu.VMEM((PULSES, WIDTH), f32),
+            pltpu.VMEM((RB, KS * T, T), bf16),
             pltpu.VMEM((STEPS, 2, HALF, WIDTH), f32),
             pltpu.VMEM((STEPS, 2, 3, HALF, WIDTH), f32),
             pltpu.VMEM((PULSES, WIDTH), f32),
@@ -439,7 +456,7 @@
         compiler_params=pltpu.CompilerParams(
             collective_id=0, has_side_effects=True, vmem_limit_bytes=60 << 20
         ),
-    )(columns, counts, history, tiles, inverse, excitation)
+    )(columns.transpose(1, 2, 0), counts.T, history, tiles, inverse, excitation)
 
 
 def solution(mesh):

time: 147 us -> 124 us (0.84)
  Pallas kernels: 143 us -> 122 us
  local copies, waits for them, and re-layouts: 4.42 us -> 1.67 us
    pallas_call x1, Pallas kernels: 143 us -> 122 us  [local(): pl.pallas_call(kernel, out_shape=jax.ShapeDtypeStruct((STEPS, PULSES, WID...]
    unnamed x3 -> x1, local copies, waits for them, and re-layouts: 4.42 us -> 1.67 us
where the time goes in v2:
time: 124 us; the launch traced here: 123 us
  Pallas kernels  122 us (98%)
  local copies, waits for them, and re-layouts  1.67 us (1%)
    pallas_call x1, Pallas kernels, local(): pl.pallas_call(kernel, out_shape=jax.ShapeDtypeStruct((STEPS, PULSES, WID...  122 us

profile of v2, /device:TPU:25, one launch (start us, length us, event | category | flops | bytes accessed | tf_op | source)
XLA Modules:
  0.0 123.5 jit_solution(14663593731688105442)
XLA Ops:
  0.0 121.8 %shard_map.64 = bf16[16,16,512]{2,1,0:T(8,128)(2,1)} custom-call(s32[4,8,16]{2,1,0:T(8,128)} %bitcast.2, s32[4,16]{1,0:T(4,128)} %bitcast.3, bf16[16,16,16384]{2,1,0:T(8,128)(2,1)} %hist_hbm.1, bf16[16,4,8,128,128]{4,3,2,1,0:T(8,128)(2,1)} %tiles_hbm.1, bf16[4,128,128]{2,1,0:T(8,128)(2,1)} %inv_hbm.1, f32[16,16,512]{2,1,0:T(8,128)} %exc_hbm.1), custom_call_target="tpu_custom_call" | custom-call | tf_op jit(solution)/shard_map/pallas_call | solution.py:432
  121.8 1.7 %copy.8 = bf16[16,16,512]{2,1,0:T(8,128)(2,1)} copy(bf16[16,16,512]{2,1,0:T(8,128)(2,1)} %shard_map.64) | data formatting | bytes 524288

commit v3 on v2

--- a/solution.py
+++ b/solution.py
@@ -20,7 +20,10 @@
 SENT = STEPS - 1
 NB = 128
 WIDTH = RB * T
+EARLY = 3
+AHEAD = 2
 NEAR = 8
+SPARE = STEPS - NEAR - 2
 
 
 def ring_hops(d, n):
@@ -32,6 +35,8 @@
     key=lambda o: -(o[0] + ring_hops(o[1], NZ) + ring_hops(o[2], NX)),
 )
 
+EVERY = OFFSETS + [(0, 0, 0)]
+
 
 def dot_t(a, b):
     return lax.dot_general(a, b, (((1,), (1,)), ((), ())), preferred_element_type=jnp.float32)
@@ -39,7 +44,7 @@
 
 def kernel(
     columns, counts, hist_hbm, tiles_hbm, inv_hbm, exc_hbm, out_ref,
-    tiles, h0, land, work, inv, exc, acc, base, first_lag, part, parts, solf, outbuf,
+    tiles, h0, land, slices, work, inv, exc, acc, soon, base, first_lag, part, parts, solf, outbuf,
     tsem, hsem, isem, esem, recv_a, recv_b, send_a, send_b,
     hrecv, slice_recv, slice_send, fwd_send, stream_send, part_send, part_recv, out_send, out_recv,
 ):
@@ -56,40 +61,39 @@
     def greet(lag, row):
         pl.semaphore_signal(barrier, inc=1, device_id=(lag, row), device_id_type=MESH)
 
-    @pl.when(g % 2 == 0)
+    @pl.when(g == 0)
     def _():
         for o in OFFSETS:
-            greet(g, peer(o))
-
-    @pl.when(g == 0)
-    def _():
+            greet(0, peer(o))
         for other in (1, 2, 3):
             greet(other, r)
 
     @pl.when(g == 1)
     def _():
         greet(0, r)
-        greet(2, partner)
+        greet(3, partner)
 
     @pl.when(g == 2)
     def _():
+        for o in EVERY:
+            greet(3, peer(o))
         greet(0, r)
-        greet(3, r)
+
+    @pl.when(g == 3)
+    def _():
+        for o in EVERY:
+            greet(2, peer(o))
+        greet(0, r)
         greet(1, partner)
-
-    @pl.when(g == 3)
-    def _():
-        greet(0, r)
-        greet(2, r)
 
     def wait_for_greetings():
         @pl.when(g % 2 == 0)
         def _():
-            pl.semaphore_wait(barrier, ROWS - 1 + 3)
+            pl.semaphore_wait(barrier, jnp.where(g == 0, ROWS - 1 + 3, ROWS + 1))
 
         @pl.when(g % 2 == 1)
         def _():
-            pl.semaphore_wait(barrier, 2)
+            pl.semaphore_wait(barrier, jnp.where(g == 1, 2, ROWS + 2))
 
     def load_block(c, carry):
         pltpu.make_async_copy(
@@ -107,6 +111,7 @@
 
     zero_block = jnp.zeros((T // 8, T), jnp.bfloat16)
     acc[...] = jnp.zeros_like(acc)
+    soon[...] = jnp.zeros_like(soon)
     for e in range(LAGS):
         h0[e, NB] = zero_block
     for tau in range(SENT):
@@ -119,10 +124,10 @@
         cs = pl.ds(RB * partner, RB)
         return pltpu.make_async_remote_copy(
             h0.at[LAGS - 1 - tau, cs],
-            land.at[tau, cs],
+            slices.at[tau],
             slice_send.at[tau],
             slice_recv.at[tau],
-            device_id=(2, partner),
+            device_id=(3, partner),
             device_id_type=MESH,
         )
 
@@ -153,17 +158,18 @@
 
             lax.fori_loop(0, SENT, one, 0)
 
-    def forward_copy(tau, o):
-        here = land.at[tau, pl.ds(RB * r, RB)]
-        return pltpu.make_async_remote_copy(
-            here, here, fwd_send.at[tau], hrecv.at[tau], device_id=(2, peer(o)), device_id_type=MESH
-        )
-
     def forward(tau):
-        here = land.at[tau, pl.ds(RB * r, RB)]
+        here = slices.at[tau]
         pltpu.make_async_copy(here, here, slice_recv.at[tau]).wait()
-        for o in OFFSETS:
-            forward_copy(tau, o).start()
+        for o in EVERY:
+            pltpu.make_async_remote_copy(
+                here,
+                land.at[tau, pl.ds(RB * r, RB)],
+                fwd_send.at[tau],
+                hrecv.at[tau],
+                device_id=(2, peer(o)),
+                device_id_type=MESH,
+            ).start()
 
     def column(l, b, k):
         return jnp.where(k < counts[b, l], columns[b, k, l], NB)
@@ -171,31 +177,45 @@
     def weights(l, b):
         return jnp.concatenate([tiles[l, b, k] for k in range(KS)], axis=1)
 
-    for quarter in range(4):
+    def row_of(s):
+        return SPARE + STEPS - 1 - s
+
+    def meet_own(l, first, entries, total, start):
+        for b in range(RB):
+            xs = [
+                h0[pl.ds(first, entries), column(l, b, k)].reshape(entries * PULSES, T)
+                for k in range(KS)
+            ]
+            got = dot_t(jnp.concatenate(xs, axis=1), weights(l, b))
+            here = (pl.ds(start, entries), slice(None), pl.ds(b * T, T))
+            total[here] += got.reshape(entries, PULSES, T)
+
+    def first_steps(l, carry):
+        pltpu.make_async_copy(tiles.at[l], tiles.at[l], tsem.at[l]).wait()
+        meet_own(l, l - 1, 2, soon, 0)
+        return carry
+
+    def quarter_of_lags(quarter):
         entries = 4 * quarter + 4
 
         def own_lag(l, carry):
-            pltpu.make_async_copy(tiles.at[l], tiles.at[l], tsem.at[l]).wait()
-            for b in range(RB):
-                xs = [
-                    h0[0:entries, column(l, b, k)].reshape(entries * PULSES, T) for k in range(KS)
-                ]
-                got = dot_t(jnp.concatenate(xs, axis=1), weights(l, b))
-                here = (pl.ds(LAGS - 1 - l, entries), slice(None), pl.ds(b * T, T))
-                acc[here] += got.reshape(entries, PULSES, T)
+            meet_own(l, 0, entries, acc, SPARE + LAGS - 1 - l)
             return carry
 
         lax.fori_loop(4 * quarter, 4 * quarter + 4, own_lag, 0)
-        if quarter == 0:
-            wait_for_greetings()
-            send_history()
-        if quarter == 2:
-
-            @pl.when(g == 2)
-            def _():
-                forward(0)
-
-
+
+    pltpu.make_async_copy(tiles.at[0], tiles.at[0], tsem.at[0]).wait()
+    meet_own(0, 0, 1, soon, 1)
+    lax.fori_loop(1, LAGS // 2, first_steps, 0)
+    wait_for_greetings()
+    send_history()
+    lax.fori_loop(LAGS // 2, 12, first_steps, 0)
+    @pl.when(g == 3)
+    def _():
+        for tau in range(1):
+            forward(tau)
+
+    lax.fori_loop(12, LAGS, first_steps, 0)
     inv_copy.wait()
     exc_copy.wait()
 
@@ -210,8 +230,9 @@
         )
 
     def send_part(s):
+        total, row = (soon, 1 - s) if isinstance(s, int) else (acc, row_of(s))
         for ch in range(2):
-            part[s, ch] = acc[STEPS - 1 - s, pl.ds(ch * HALF, HALF), :]
+            part[s, ch] = total[row, pl.ds(ch * HALF, HALF), :]
         for ch in range(2):
             part_copy(s, ch).start()
 
@@ -219,36 +240,62 @@
     def _():
         send_part(0)
 
+        @pl.when(g == 3)
+        def _():
+            for tau in range(1, AHEAD):
+                forward(tau)
+
+        def meet(lag, first, entries, total, start):
+            for b in range(RB):
+                xs = [
+                    work[pl.ds(first, entries), 0, column(lag - 1, b, k)].reshape(entries * PULSES, T)
+                    for k in range(KS)
+                ]
+                got = dot_t(jnp.concatenate(xs, axis=1), weights(lag - 1, b))
+                here = (pl.ds(start, entries), slice(None), pl.ds(b * T, T))
+                total[here] += got.reshape(entries, PULSES, T)
+
+        def meet_later(lag, first, entries):
+            meet(lag, first, entries, acc, SPARE + 1 - lag + first)
+
+        def arrive(tau):
+            pltpu.make_async_copy(land.at[tau], land.at[tau], hrecv.at[tau]).wait()
+            work[SENT - 1 - tau, 0, pl.ds(0, NB)] = land[tau]
+
+        def go_on(tau):
+            @pl.when((g == 3) & (tau < SENT - AHEAD))
+            def _():
+                forward(tau + AHEAD)
+
+            def near(lag, carry):
+                meet_later(lag, SENT - 1 - (tau + 2 - lag), 1)
+                return carry
+
+            @pl.when(tau < SENT - 1)
+            def _():
+                lax.fori_loop(2, jnp.minimum(NEAR, tau + 2) + 1, near, 0)
+
+            @pl.when((tau >= NEAR - 1) & (tau < SENT - 1))
+            def _():
+                meet_later(tau + 2, NEAR, SENT - NEAR)
+
+        for quarter in range(EARLY):
+            quarter_of_lags(quarter)
+        arrive(0)
+        meet(1, SENT - 1, 1, soon, 0)
+        send_part(1)
+        for quarter in range(EARLY, 4):
+            quarter_of_lags(quarter)
+        go_on(jnp.int32(0))
+
         def entry(tau, carry):
-            @pl.when((g == 2) & (tau < SENT - 1))
-            def _():
-                forward(tau + 1)
-
-            @pl.when(g == 2)
-            def _():
-                arrived = land.at[tau, pl.ds(0, NB - RB)]
-                pltpu.make_async_copy(arrived, arrived, hrecv.at[tau]).wait()
-
-            @pl.when(g != 2)
-            def _():
-                pltpu.make_async_copy(land.at[tau], land.at[tau], hrecv.at[tau]).wait()
-
-            work[tau, 0, pl.ds(0, NB)] = land[tau]
-
-            def push(lag, carry):
-                for b in range(RB):
-                    xs = [work[tau, 0, column(lag - 1, b, k)] for k in range(KS)]
-                    got = dot_t(jnp.concatenate(xs, axis=1), weights(lag - 1, b))
-                    here = (STEPS - 1 - (tau + lag), slice(None), pl.ds(b * T, T))
-                    acc[here] += got
-                return carry
-
-            push(1, 0)
+            arrive(tau)
+            meet_later(1, SENT - 1 - tau, 1)
             send_part(tau + 1)
-            lax.fori_loop(2, STEPS - tau, push, 0)
-            return carry
-
-        lax.fori_loop(0, SENT, entry, 0)
+            go_on(tau)
+            return carry
+
+        lax.fori_loop(1, SENT, entry, 0)
 
     low = lax.broadcasted_iota(jnp.int32, (2 * HALF, T), 0) < HALF
     keep_low = jnp.where(low, 1.0, 0.0).astype(jnp.bfloat16)
@@ -276,10 +323,14 @@
     def set_base(s):
         pltpu.make_async_copy(parts.at[s], parts.at[s], part_recv.at[s]).wait()
         other = [parts[s, ch, 0] + parts[s, ch, 1] + parts[s, ch, 2] for ch in range(2)]
-        field = exc[s] - (acc[STEPS - 1 - s] + jnp.concatenate(other, axis=0))
-        rhs = field.astype(jnp.bfloat16)
+        own = soon[1 - s] if isinstance(s, int) else acc[row_of(s)]
+        field = exc[s] - (own + jnp.concatenate(other, axis=0))
+        high = field.astype(jnp.bfloat16)
+        rest = (field - high.astype(jnp.float32)).astype(jnp.bfloat16)
+        rhs = jnp.concatenate([high, rest], axis=0)
         for b in range(RB):
-            base[:, pl.ds(b * T, T)] = dot_t(rhs[:, b * T : (b + 1) * T], inv[b])
+            got = dot_t(rhs[:, b * T : (b + 1) * T], inv[b])
+            base[:, pl.ds(b * T, T)] = got[0:PULSES] + got[PULSES : 2 * PULSES]
 
     def chain(s, ch, first):
         if not first:
@@ -334,7 +385,7 @@
                 xa = jnp.concatenate([work[tau, 0, c] for c in cs], axis=1)
                 xb = jnp.concatenate([work[tau, 1, c] for c in cs], axis=1)
                 got = dot_t(jnp.concatenate([xa, xb], axis=0), weights(lag - 1, b))
-                here = (STEPS - 1 - target, slice(None), pl.ds(b * T, T))
+                here = (row_of(target), slice(None), pl.ds(b * T, T))
                 acc[here] += jnp.concatenate(
                     [folded(got[0 : 2 * HALF]), folded(got[2 * HALF : 4 * HALF])], axis=0
                 )
@@ -350,9 +401,13 @@
                     tiles[0, b, k], inv[b], (((0,), (1,)), ((), ())), preferred_element_type=jnp.float32
                 )
                 first_lag[b, pl.ds(k * T, T), :] = product.astype(jnp.bfloat16)
+        quarter_of_lags(0)
+        quarter_of_lags(1)
         set_base(0)
         chain(0, 0, True)
         chain(0, 1, True)
+        quarter_of_lags(2)
+        quarter_of_lags(3)
         hand_out(0)
         set_base(1)
 
@@ -412,11 +467,10 @@
 
         lax.fori_loop(0, SENT, drain, 0)
 
-    @pl.when(g == 2)
+    @pl.when(g == 3)
     def _():
         def drain(tau, carry):
-            sent = land.at[tau, pl.ds(0, NB - RB)]
-            pltpu.make_async_copy(sent, sent, fwd_send.at[tau]).wait()
+            pltpu.make_async_copy(land.at[tau], land.at[tau], fwd_send.at[tau]).wait()
             return carry
 
         lax.fori_loop(0, SENT, drain, 0)
@@ -438,10 +492,12 @@
             pltpu.VMEM((LAGS, RB, KS, T, T), bf16),
             pltpu.VMEM((LAGS, NB + 1, PULSES, T), bf16),
             pltpu.VMEM((SENT, NB, PULSES, T), bf16),
+            pltpu.VMEM((SENT, RB, PULSES, T), bf16),
             pltpu.VMEM((SENT, 2, NB + 1, PULSES, T), bf16),
             pltpu.VMEM((RB, T, T), bf16),
             pltpu.VMEM((STEPS, PULSES, WIDTH), f32),
-            pltpu.VMEM((STEPS + 3, PULSES, WIDTH), f32),
+            pltpu.VMEM((SPARE + STEPS + 3, PULSES, WIDTH), f32),
+            pltpu.VMEM((2, PULSES, WIDTH), f32),
             pltpu.VMEM((PULSES, WIDTH), f32),
             pltpu.VMEM((RB, KS * T, T), bf16),
             pltpu.VMEM((STEPS, 2, HALF, WIDTH), f32),

time: 124 us -> 123 us (level)
  no operation moved by 1% of the time
where the time goes in v3:
time: 123 us
  Pallas kernels  121 us (98%)
  local copies, waits for them, and re-layouts  1.67 us (1%)
    pallas_call x1, Pallas kernels, local(): pl.pallas_call(kernel, out_shape=jax.ShapeDtypeStruct((STEPS, PULSES, WID...  121 us

profile of v3, /device:TPU:25, one launch (start us, length us, event | category | flops | bytes accessed | tf_op | source)
XLA Modules:
  0.0 122.6 jit_solution(12949582611792401415)
XLA Ops:
  0.0 120.9 %shard_map.64 = bf16[16,16,512]{2,1,0:T(8,128)(2,1)} custom-call(s32[4,8,16]{2,1,0:T(8,128)} %bitcast.2, s32[4,16]{1,0:T(4,128)} %bitcast.3, bf16[16,16,16384]{2,1,0:T(8,128)(2,1)} %hist_hbm.1, bf16[16,4,8,128,128]{4,3,2,1,0:T(8,128)(2,1)} %tiles_hbm.1, bf16[4,128,128]{2,1,0:T(8,128)(2,1)} %inv_hbm.1, f32[16,16,512]{2,1,0:T(8,128)} %exc_hbm.1), custom_call_target="tpu_custom_call" | custom-call | tf_op jit(solution)/shard_map/pallas_call | solution.py:486
  120.9 1.7 %copy.8 = bf16[16,16,512]{2,1,0:T(8,128)(2,1)} copy(bf16[16,16,512]{2,1,0:T(8,128)(2,1)} %shard_map.64) | data formatting | bytes 524288
